TPU v7x, 32 devices: a whole 2x2x4 slice. The times are simulated.
32 devices in a mesh: dp: 8 (over y, x, core), blk: 4 (over z).
Axes of the slice: x: 2, y: 2, z: 4, core: 2. Of those that a mesh axis runs over, the one named last changes fastest.
Arguments:
- layer_input: bfloat16 [4096, 2048], P(('dp', 'blk')), may hold values from -6 to 6
- out_grad: bfloat16 [4096, 2048], P(('dp', 'blk')), may hold values from -6 to 6
- expert_ids: int32 [4096, 2], P(('dp', 'blk')), may hold values from 0 to 7, all different within a row; in each aligned block of 128 rows (0 to 127, 128 to 255, ...) at most 40 rows name the same one
- combine: float32 [4096, 2], P(('dp', 'blk')), may hold values from 0.1 to 1
- bucket_ids: int32 [4096, 4], P(('dp', 'blk')), may hold values from 0 to 1023, as said below
- w_gate: bfloat16 [4, 8, 2048, 352], P('blk', 'dp'), may hold values from -0.125 to 0.125
- w_up: bfloat16 [4, 8, 2048, 352], P('blk', 'dp'), may hold values from -0.125 to 0.125
- w_down: bfloat16 [4, 8, 352, 2048], P('blk', 'dp'), may hold values from -0.15625 to 0.15625
Outputs:
- grad_gate: bfloat16 [4, 8, 2048, 352], P('blk', 'dp')
- grad_up: bfloat16 [4, 8, 2048, 352], P('blk', 'dp')
- grad_down: bfloat16 [4, 8, 352, 2048], P('blk', 'dp')
- ngram_grad: float32 [4, 1024, 2048], P(None, 'dp', 'blk')
Inputs may be any that keep to these rules, and one draw needn't show every extreme that they name: `expert_ids`: within the 128 rows of one device (aligned blocks of rows) no expert is named more than 40 times. `bucket_ids`: within the 128 rows of one device (aligned blocks), at most 128 of the ids lie in any one range [128 * i, 128 * (i + 1)); on every device one such range, the same for all devices, holds exactly 128.
All inputs are finite; a program needn't handle non-finite values.
Results may differ from a plain program's by a relative error of at most 0.009.
Values may be sent and summed in bfloat16 or wider, within the bound.
A program may use at most 128 MiB of HBM per device.

v0:
```python
import jax
import jax.numpy as jnp
from jax import lax
from jax.sharding import PartitionSpec as P

NHASH = 4
SHARDS = 4
BUCK_DEV = 128


def expert_block(rows_x, rows_g, gate_w, up_w, down_w):
    gate = jnp.dot(rows_x, gate_w, preferred_element_type=jnp.float32)
    upper = jnp.dot(rows_x, up_w, preferred_element_type=jnp.float32)
    sigma = jax.nn.sigmoid(gate)
    active = gate * sigma
    hidden = (active * upper).astype(jnp.bfloat16)
    d_hidden = lax.dot_general(
        rows_g, down_w, (((1,), (1,)), ((), ())), preferred_element_type=jnp.float32
    )
    d_up = (d_hidden * active).astype(jnp.bfloat16)
    d_gate = (d_hidden * upper * sigma * (1.0 + gate * (1.0 - sigma))).astype(jnp.bfloat16)
    d_rows = lax.dot_general(
        d_gate, gate_w, (((1,), (1,)), ((), ())), preferred_element_type=jnp.float32
    )
    d_rows = d_rows + lax.dot_general(
        d_up, up_w, (((1,), (1,)), ((), ())), preferred_element_type=jnp.float32
    )
    grad_down = lax.dot_general(
        hidden, rows_g, (((0,), (0,)), ((), ())), preferred_element_type=jnp.float32
    )
    grad_gate = lax.dot_general(
        rows_x, d_gate, (((0,), (0,)), ((), ())), preferred_element_type=jnp.float32
    )
    grad_up = lax.dot_general(
        rows_x, d_up, (((0,), (0,)), ((), ())), preferred_element_type=jnp.float32
    )
    return (d_rows.astype(jnp.bfloat16), grad_gate, grad_up, grad_down)


def place_rows(category, category_total, capacity):
    onehot = (category[:, None] == jnp.arange(category_total, dtype=jnp.int32)[None, :]).astype(
        jnp.int32
    )
    running = jnp.cumsum(onehot, axis=0)
    position = jnp.sum(running * onehot, axis=1) - 1
    return category * capacity + position


def on_device(layer_input, out_grad, expert_ids, combine, bucket_ids, w_gate, w_up, w_down):
    group_count = lax.axis_size("blk")
    member_count = lax.axis_size("dp")
    quad_count = member_count // SHARDS
    expert_count = group_count * quad_count
    token_count, width = layer_input.shape
    capacity = 5 * token_count // (2 * expert_count)
    pair_count = token_count * 2
    slots = place_rows(expert_ids.reshape(pair_count), expert_count, capacity)
    filler = (
        jnp.full((expert_count * capacity,), -1, jnp.int32)
        .at[slots]
        .set(jnp.arange(pair_count, dtype=jnp.int32))
    )
    present = filler >= 0
    source = jnp.maximum(filler, 0)
    weighted = (
        (combine[:, :, None] * out_grad[:, None, :].astype(jnp.float32))
        .astype(jnp.bfloat16)
        .reshape(pair_count, width)
    )
    send_rows = jnp.where(present[:, None], layer_input[source // 2], jnp.zeros((), jnp.bfloat16))
    send_grads = jnp.where(present[:, None], weighted[source], jnp.zeros((), jnp.bfloat16))
    send_rows = send_rows.reshape(group_count, quad_count * capacity, width)
    send_grads = send_grads.reshape(group_count, quad_count * capacity, width)
    group_rows, group_grads = (
        lax.all_to_all(send_rows, "blk", split_axis=0, concat_axis=0, tiled=True),
        lax.all_to_all(send_grads, "blk", split_axis=0, concat_axis=0, tiled=True),
    )

    def copies(values):
        folded = values.reshape(group_count, quad_count, 1, capacity * width)
        spread = jnp.broadcast_to(folded, (group_count, quad_count, SHARDS, capacity * width))
        return spread.reshape(group_count, member_count * capacity, width)

    member_rows, member_grads = (
        lax.all_to_all(copies(group_rows), "dp", split_axis=1, concat_axis=1, tiled=True),
        lax.all_to_all(copies(group_grads), "dp", split_axis=1, concat_axis=1, tiled=True),
    )
    total_rows = group_count * member_count * capacity
    flat_rows = member_rows.reshape(total_rows, width)
    flat_grads = member_grads.reshape(total_rows, width)
    gate_w = w_gate[0, 0]
    up_w = w_up[0, 0]
    down_w = w_down[0, 0]
    d_rows, grad_g, grad_u, grad_d = expert_block(flat_rows, flat_grads, gate_w, up_w, down_w)
    partials = d_rows.reshape(group_count, member_count * capacity, width)
    returned = lax.all_to_all(partials, "dp", split_axis=1, concat_axis=1, tiled=True)
    quarters = returned.reshape(group_count, quad_count, SHARDS, capacity * width).astype(
        jnp.float32
    )
    combined = (
        jnp.sum(quarters, axis=2)
        .astype(jnp.bfloat16)
        .reshape(group_count, quad_count * capacity, width)
    )
    arrived = lax.all_to_all(combined, "blk", split_axis=0, concat_axis=0, tiled=True).reshape(
        expert_count * capacity, width
    )
    slot_grads = arrived[slots].reshape(token_count, 2, width).astype(jnp.float32)
    emb_grad = (out_grad.astype(jnp.float32) + slot_grads[:, 0] + slot_grads[:, 1]).astype(
        jnp.bfloat16
    )
    pair_total = token_count * NHASH
    bucket_flat = bucket_ids.reshape(pair_total)
    owner = bucket_flat // BUCK_DEV
    owner_cap = 2 * pair_total // member_count
    owner_slots = place_rows(owner, member_count, owner_cap)
    owner_fill = (
        jnp.full((member_count * owner_cap,), -1, jnp.int32)
        .at[owner_slots]
        .set(jnp.arange(pair_total, dtype=jnp.int32))
    )
    owner_live = owner_fill >= 0
    owner_source = jnp.maximum(owner_fill, 0)
    table_rows = jnp.where(
        owner_live[:, None], emb_grad[owner_source // NHASH], jnp.zeros((), jnp.bfloat16)
    )
    table_keys = jnp.where(
        owner_live, owner_source % NHASH * BUCK_DEV + bucket_flat[owner_source] % BUCK_DEV, 0
    )
    piece = width // group_count
    rows_whole = table_rows.reshape(member_count, owner_cap, width)
    keys_whole = table_keys.reshape(member_count, owner_cap)
    got_rows, got_keys = (
        lax.all_to_all(rows_whole, "dp", split_axis=0, concat_axis=0, tiled=True),
        lax.all_to_all(keys_whole, "dp", split_axis=0, concat_axis=0, tiled=True),
    )
    owner_sums = jax.ops.segment_sum(
        got_rows.reshape(-1, width).astype(jnp.float32),
        got_keys.reshape(-1),
        num_segments=NHASH * BUCK_DEV,
    )
    accum = lax.psum_scatter(
        owner_sums.astype(jnp.bfloat16), "blk", scatter_dimension=1, tiled=True
    ).astype(jnp.float32)
    ngram_grad = accum.reshape(NHASH, BUCK_DEV, piece)
    return (
        grad_g.astype(jnp.bfloat16)[None, None],
        grad_u.astype(jnp.bfloat16)[None, None],
        grad_d.astype(jnp.bfloat16)[None, None],
        ngram_grad,
    )


def solution(mesh):
    return jax.shard_map(
        on_device,
        mesh=mesh,
        in_specs=(
            P(("dp", "blk"), None),
            P(("dp", "blk"), None),
            P(("dp", "blk"), None),
            P(("dp", "blk"), None),
            P(("dp", "blk"), None),
            P("blk", "dp", None, None),
            P("blk", "dp", None, None),
            P("blk", "dp", None, None),
        ),
        out_specs=(
            P("blk", "dp", None, None),
            P("blk", "dp", None, None),
            P("blk", "dp", None, None),
            P(None, "dp", "blk"),
        ),
        check_vma=False,
    )
```

profile of v0, /device:TPU:0, one launch (start us, length us, event | category | flops | bytes accessed | tf_op | source)
XLA Modules:
  0.0 528.6 jit_solution(7279874371449634671)
XLA Ops:
  30.7 37.6 %all_to_all.44 = bf16[4,80,2048]{2,1,0:T(8,128)(2,1)} all-to-all(bf16[4,80,2048]{2,1,0:T(8,128)(2,1)S(1)} %get-tuple-element.13), channel_id=1, replica_groups=mesh['dp'=8,'blk'=4] {'blk'}, dimensions={0} | all-to-all | bytes 2621440 | tf_op jit(solution)/shard_map/all_to_all | solution.py:75
  76.3 5.0 broadcast_in_dim.95
  81.3 8.8 %reshape.264 = bf16[4,320,2048]{2,1,0:T(8,128)(2,1)} reshape(bf16[4,2,4,81920]{3,2,1,0:T(4,128)(2,1)} %broadcast_in_dim.95) | data formatting | bytes 10485760 | tf_op jit(solution)/shard_map/reshape | solution.py:82
  90.1 8.9 %copy.36 = bf16[4,320,2048]{2,0,1:T(4,128)(2,1)} copy(bf16[4,320,2048]{2,1,0:T(8,128)(2,1)} %reshape.264) | data formatting | bytes 10485760 | tf_op jit(solution)/shard_map/reshape | solution.py:82
  109.8 5.0 broadcast_in_dim.98
  114.9 8.9 %reshape.266 = bf16[4,320,2048]{2,1,0:T(8,128)(2,1)} reshape(bf16[4,2,4,81920]{3,2,1,0:T(4,128)(2,1)} %broadcast_in_dim.98) | data formatting | bytes 10485760 | tf_op jit(solution)/shard_map/reshape | solution.py:82
  123.7 8.9 %copy.39 = bf16[4,320,2048]{2,0,1:T(4,128)(2,1)} copy(bf16[4,320,2048]{2,1,0:T(8,128)(2,1)} %reshape.266) | data formatting | bytes 10485760 | tf_op jit(solution)/shard_map/reshape | solution.py:82
  132.6 35.4 %all-to-all-done.1 = bf16[4,320,2048]{2,0,1:T(4,128)(2,1)} async-done(((bf16[4,320,2048]{2,0,1:T(4,128)(2,1)}), bf16[4,320,2048]{2,0,1:T(4,128)(2,1)}, u32[]{:S(2)}, u32[]{:S(2)}) %all-to-all-start.1) | async-done | bytes 5242912 | tf_op jit(solution)/shard_map/all_to_all | solution.py:85
  172.9 5.4 %copy.37 = bf16[4,320,2048]{2,1,0:T(8,128)(2,1)S(1)} copy(bf16[4,320,2048]{2,0,1:T(4,128)(2,1)} %all-to-all-done.1) | data formatting | bytes 10485760 | tf_op jit(solution)/shard_map/all_to_all | solution.py:85
  184.9 48.1 %all-to-all-done.3 = bf16[4,320,2048]{2,0,1:T(4,128)(2,1)} async-done(((bf16[4,320,2048]{2,0,1:T(4,128)(2,1)}), bf16[4,320,2048]{2,0,1:T(4,128)(2,1)}, u32[]{:S(2)}, u32[]{:S(2)}) %all-to-all-start.3) | async-done | bytes 5242912 | tf_op jit(solution)/shard_map/all_to_all | solution.py:86
  233.0 5.5 %copy.40 = bf16[4,320,2048]{2,1,0:T(8,128)(2,1)S(1)} copy(bf16[4,320,2048]{2,0,1:T(4,128)(2,1)} %all-to-all-done.3) | data formatting | bytes 10485760 | tf_op jit(solution)/shard_map/all_to_all | solution.py:86
  247.7 6.3 %copy.44 = bf16[4,320,2048]{2,0,1:T(4,128)(2,1)} copy(bf16[4,320,2048]{2,1,0:T(8,128)(2,1)S(1)} %bitcast.77) | data formatting | bytes 10485760 | tf_op jit(solution)/shard_map/reshape | solution.py:95
  259.2 60.1 %all-to-all-done.5 = bf16[4,320,2048]{2,0,1:T(4,128)(2,1)} async-done(((bf16[4,320,2048]{2,0,1:T(4,128)(2,1)}), bf16[4,320,2048]{2,0,1:T(4,128)(2,1)}, u32[]{:S(2)}, u32[]{:S(2)}) %all-to-all-start.5) | async-done | bytes 5242912 | tf_op jit(solution)/shard_map/all_to_all | solution.py:96
  319.3 7.6 %copy.45 = bf16[4,320,2048]{2,1,0:T(8,128)(2,1)} copy(bf16[4,320,2048]{2,0,1:T(4,128)(2,1)} %all-to-all-done.5) | data formatting | bytes 10485760 | tf_op jit(solution)/shard_map/all_to_all | solution.py:96
  326.9 8.6 %reshape.273 = bf16[4,2,4,81920]{3,2,1,0:T(4,128)(2,1)} reshape(bf16[4,320,2048]{2,1,0:T(8,128)(2,1)} %copy.45) | data formatting | bytes 10485760 | tf_op jit(solution)/shard_map/reshape | solution.py:97
  335.5 10.1 %reduce_sum.32 = bf16[4,2,81920]{2,1,0:T(2,128)(2,1)S(1)} reduce(bf16[4,2,4,81920]{3,2,1,0:T(4,128)(2,1)} %reshape.273, bf16[]{:T(256)} %constant.97.clone.1), dimensions={2}, to_apply=%region_8.9 | reduce | flops 1966080 | bytes 6553602 | tf_op jit(solution)/shard_map/reduce_sum | solution.py:101
  356.0 6.9 %gather_fusion.2 = s32[1024]{0:T(1024)S(1)} fusion(s32[512]{0:T(512)S(1)} %reshape.269, s32[1024]{0:T(1024)S(1)} %get-tuple-element.9), kind=kCustom, calls=%fused_computation.2 | custom fusion | bytes 12288 | tf_op jit(solution)/shard_map/gather | solution.py:128
  363.5 16.9 %all-to-all-done.6 = bf16[4,80,2048]{2,1,0:T(8,128)(2,1)S(1)} async-done(((bf16[4,80,2048]{2,1,0:T(8,128)(2,1)}), bf16[4,80,2048]{2,1,0:T(8,128)(2,1)S(1)}, u32[]{:S(2)}, u32[]{:S(2)}) %all-to-all-start.6) | async-done | bytes 1310752 | tf_op jit(solution)/shard_map/all_to_all | solution.py:105
  380.4 5.0 all-to-all-start.4
  392.7 6.0 %gather_fusion.4 = bf16[1024,2048]{1,0:T(8,128)(2,1)} fusion(bf16[128,2048]{1,0:T(8,128)(2,1)S(1)} %fusion.17, s32[1024]{0:T(1024)S(1)} %get-tuple-element.8), kind=kCustom, calls=%fused_computation.4 | custom fusion | bytes 8392704 | tf_op jit(solution)/shard_map/gather | solution.py:125
  403.3 53.8 %all_to_all.45 = bf16[8,128,2048]{2,1,0:T(8,128)(2,1)} all-to-all(bf16[8,128,2048]{2,1,0:T(8,128)(2,1)} %broadcast_select_fusion), channel_id=1, replica_groups=mesh['dp'=8,'blk'=4] {'dp'}, dimensions={0} | all-to-all | bytes 8388608 | tf_op jit(solution)/shard_map/all_to_all | solution.py:134
  457.1 16.9 %scatter_custom_fusion.2 = f32[512,2048]{1,0:T(8,128)} fusion(s32[1024]{0:T(1024)S(1)} %bitcast.97, bf16[1024,2048]{1,0:T(8,128)(2,1)} %bitcast.79, f32[]{:T(128)} %constant.99.clone.1), kind=kCustom, calls=%fused_computation.9 | custom fusion | flops 4194304 | bytes 8388612 | tf_op jit(solution)/shard_map/scatter-add | solution.py:137
  479.1 6.1 %fusion.4 = bf16[1,1,2048,352]{2,3,1,0:T(8,128)(2,1)} fusion(bf16[1280,352]{0,1:T(8,128)(2,1)S(1)} %copy-done.8, bf16[1280,2048]{1,0:T(8,128)(2,1)} %bitcast.82), kind=kOutput, calls=%fused_computation.17 | convolution fusion | flops 1846214656 | bytes 7585792 | tf_op jit(solution)/shard_map/dot_general | solution.py:34
  491.8 27.4 %reduce-scatter.2.cloned.1.call-done = bf16[512,512]{1,0:T(8,128)(2,1)} async-done(((bf16[512,2048]{1,0:T(8,128)(2,1)}), bf16[512,512]{1,0:T(8,128)(2,1)}) %reduce-scatter.2.cloned.1.call-update) | async-done | bytes 524304 | tf_op jit(solution)/shard_map/reduce_scatter | solution.py:142
  (118 shorter events, 104.6 us)
Async XLA Ops:
  7.2 171.1 %copy-start = (bf16[1,1,2048,352]{2,3,1,0:T(8,128)(2,1)S(1)}, bf16[1,1,2048,352]{2,3,1,0:T(8,128)(2,1)}, u32[]{:S(2)}) copy-start(bf16[1,1,2048,352]{2,3,1,0:T(8,128)(2,1)} %param.13) | copy-start | bytes 4325380
  16.2 3.7 copy-start.2
  68.3 34.5 %all-to-all-start.2 = ((bf16[4,80,2048]{2,1,0:T(8,128)(2,1)}), bf16[4,80,2048]{2,1,0:T(8,128)(2,1)S(1)}, u32[]{:S(2)}, u32[]{:S(2)}) async-start(bf16[4,80,2048]{2,1,0:T(8,128)(2,1)} %get-tuple-element.12), calls=%async_computation.2 | async-start | bytes 2621440 | tf_op jit(solution)/shard_map/all_to_all | solution.py:76
  102.8 65.2 %all-to-all-start.1 = ((bf16[4,320,2048]{2,0,1:T(4,128)(2,1)}), bf16[4,320,2048]{2,0,1:T(4,128)(2,1)}, u32[]{:S(2)}, u32[]{:S(2)}) async-start(bf16[4,320,2048]{2,0,1:T(4,128)(2,1)} %copy.36), calls=%async_computation.1 | async-start | bytes 10485760 | tf_op jit(solution)/shard_map/all_to_all | solution.py:85
  168.0 65.1 %all-to-all-start.3 = ((bf16[4,320,2048]{2,0,1:T(4,128)(2,1)}), bf16[4,320,2048]{2,0,1:T(4,128)(2,1)}, u32[]{:S(2)}, u32[]{:S(2)}) async-start(bf16[4,320,2048]{2,0,1:T(4,128)(2,1)} %copy.39), calls=%async_computation.3 | async-start | bytes 10485760 | tf_op jit(solution)/shard_map/all_to_all | solution.py:86
  178.3 3.4 copy-start.3
  178.3 3.3 copy-start.6
  233.0 5.5 %copy-start.12 = (bf16[1,1,352,2048]{3,2,1,0:T(8,128)(2,1)S(1)}, bf16[1,1,352,2048]{3,2,1,0:T(8,128)(2,1)}, u32[]{:S(2)}) copy-start(bf16[1,1,352,2048]{3,2,1,0:T(8,128)(2,1)} %param.15) | copy-start | bytes 4325380
  233.0 5.5 %copy-start.13 = (f32[1280,352]{0,1:T(8,128)S(1)}, f32[1280,352]{0,1:T(8,128)}, u32[]{:S(2)}) copy-start(f32[1280,352]{0,1:T(8,128)} %fusion.9) | copy-start | bytes 5406724
  233.0 5.6 %copy-start.15 = (f32[1280,352]{0,1:T(8,128)S(1)}, f32[1280,352]{0,1:T(8,128)}, u32[]{:S(2)}) copy-start(f32[1280,352]{0,1:T(8,128)} %fusion.12) | copy-start | bytes 5406724
  241.1 3.4 copy-start.9
  241.1 3.4 copy-start.7
  254.0 5.0 copy-start.11
  254.0 65.3 %all-to-all-start.5 = ((bf16[4,320,2048]{2,0,1:T(4,128)(2,1)}), bf16[4,320,2048]{2,0,1:T(4,128)(2,1)}, u32[]{:S(2)}, u32[]{:S(2)}) async-start(bf16[4,320,2048]{2,0,1:T(4,128)(2,1)} %copy.44), calls=%async_computation.5 | async-start | bytes 10485760 | tf_op jit(solution)/shard_map/all_to_all | solution.py:96
  348.0 32.4 %all-to-all-start.6 = ((bf16[4,80,2048]{2,1,0:T(8,128)(2,1)}), bf16[4,80,2048]{2,1,0:T(8,128)(2,1)S(1)}, u32[]{:S(2)}, u32[]{:S(2)}) async-start(bf16[4,80,2048]{2,1,0:T(8,128)(2,1)} %reshape.274), calls=%async_computation.6 | async-start | bytes 2621440 | tf_op jit(solution)/shard_map/all_to_all | solution.py:105
  380.4 23.0 %all-to-all-start.4 = ((s32[8,1,128]{2,1,0:T(1,128)}), s32[8,1,128]{2,1,0:T(1,128)S(1)}, u32[]{:S(2)}, u32[]{:S(2)}) async-start(s32[8,1,128]{2,1,0:T(1,128)} %bitcast.18), calls=%async_computation.4 | async-start | bytes 8192 | tf_op jit(solution)/shard_map/all_to_all | solution.py:135
  385.3 133.9 %reduce-scatter.2.cloned.1.call-start = ((), (), s32[]{:S(2)}) async-start(), calls=%async_computation.9 | async-start | bytes 2621440 | tf_op jit(solution)/shard_map/reduce_scatter | solution.py:142
  474.0 11.2 %slice-start = ((s8[5242880]{0:T(1024)(128)(4,1)}), s8[1048576]{0:T(1024)(128)(4,1)S(1)}, s32[]{:S(2)}) async-start(s8[5242880]{0:T(1024)(128)(4,1)} %bitcast.83), calls=%async_computation.10 | async-start | bytes 2097152
  479.1 6.1 %slice-start.1 = ((s8[5242880]{0:T(1024)(128)(4,1)}), s8[4194304]{0:T(1024)(128)(4,1)S(1)}, s32[]{:S(2)}) async-start(s8[5242880]{0:T(1024)(128)(4,1)} %bitcast.83), calls=%async_computation.11 | async-start | bytes 8388608
  479.1 6.1 %copy-start.10 = (bf16[1280,352]{0,1:T(8,128)(2,1)S(1)}, bf16[1280,352]{0,1:T(8,128)(2,1)}, u32[]{:S(2)}) copy-start(bf16[1280,352]{0,1:T(8,128)(2,1)} %copy-done.9) | copy-start | bytes 2703364
  479.1 9.4 %slice-start.2 = ((s8[5242880]{0:T(1024)(128)(4,1)}), s8[4194304]{0:T(1024)(128)(4,1)S(1)}, s32[]{:S(2)}) async-start(s8[5242880]{0:T(1024)(128)(4,1)} %bitcast.87), calls=%async_computation.12 | async-start | bytes 8388608
  485.2 3.2 slice-start.3
  485.3 3.2 copy-start.14
  488.5 32.8 %copy-start.1 = (bf16[1,1,2048,352]{2,3,1,0:T(8,128)(2,1)S(1)}, bf16[1,1,2048,352]{2,3,1,0:T(8,128)(2,1)}, u32[]{:S(2)}) copy-start(bf16[1,1,2048,352]{2,3,1,0:T(8,128)(2,1)} %param.13) | copy-start | bytes 4325380
  (4 other events, 8.6 us)
Sparse Core Ops, SparseCore 0:
  478.1 41.0 reduce-scatter.1
where the time goes:
time: 535 us; the launch traced here: 529 us
  waiting for transfers between devices  192 us (36%)
  local copies, waits for them, and re-layouts  128 us (24%)
  blocking collectives  91.4 us (17%)
  other arithmetic  46.9 us (9%)
  matrix products  28.1 us (5%)
  starting transfers between devices  27.5 us (5%)
  between operations  14.9 us (3%)
    all_to_all x1, waiting for transfers between devices, on_device(): lax.all_to_all(partials, 'dp', split_axis=1, concat_axis=1, tiled=True)  60.1 us
    all_to_all x1, blocking collectives, on_device(): lax.all_to_all(rows_whole, 'dp', split_axis=0, concat_axis=0, tiled=True)  53.8 us
    all_to_all x1, waiting for transfers between devices, on_device(): lax.all_to_all(copies(group_grads), 'dp', split_axis=1, concat_axis=1, ti...  48.1 us
    all_to_all x1, blocking collectives, on_device(): lax.all_to_all(send_rows, 'blk', split_axis=0, concat_axis=0, tiled=True)  37.6 us
    reshape x4, local copies, waits for them, and re-layouts, copies(): return spread.reshape(group_count, member_count * capacity, width)  35.4 us
    all_to_all x1, waiting for transfers between devices, on_device(): lax.all_to_all(copies(group_rows), 'dp', split_axis=1, concat_axis=1, til...  35.4 us
    reduce_scatter x1, waiting for transfers between devices, on_device(): lax.psum_scatter(owner_sums.astype(jnp.bfloat16), 'blk', scatter_dimensio...  27.4 us
    scatter-add x1, other arithmetic, on_device(): jax.ops.segment_sum(got_rows.reshape(-1, width).astype(jnp.float32), got_...  16.9 us
  transfers between devices with their start and end apart: 7, of which 6 were waited for; matrix products, arithmetic and copies ran while one was open for 20% of the time, Pallas kernels for 0%

commit v1 on v0

v1 whole, which is shorter than its diff:
```python
import jax
import jax.numpy as jnp
from jax import lax
from jax.sharding import Mesh, PartitionSpec as P

NHASH = 4
SHARDS = 4
BUCK_DEV = 128
F32 = jnp.float32
BF16 = jnp.bfloat16


def dot(a, b, ca, cb):
    return lax.dot_general(a, b, (((ca,), (cb,)), ((), ())), preferred_element_type=F32)


def slot_places(ids, quads, groups, capacity):
    tokens = ids.shape[0]
    expert_count = quads * groups
    dest = (ids % quads) * groups + ids // quads
    hot = (dest[:, :, None] == jnp.arange(expert_count)[None, None, :]).astype(F32)
    per_token = hot.sum(axis=1)
    before = jnp.tril(jnp.ones((tokens, tokens), F32), -1) @ per_token
    position = (hot * before[:, None, :]).sum(axis=2).astype(jnp.int32)
    return dest * capacity + position


def on_device(layer_input, out_grad, expert_ids, combine, bucket_ids, w_gate, w_up, w_down):
    groups = lax.axis_size("blk")
    quads = lax.axis_size("quad")
    experts = groups * quads
    tokens, width = layer_input.shape
    capacity = 5 * tokens // (2 * experts)
    piece = width // groups
    total = experts * capacity

    all_ids = lax.all_gather(expert_ids, "blk")
    all_buckets = lax.all_gather(bucket_ids, ("quad", "shard", "blk"), tiled=True)
    grad_pieces = lax.all_to_all(
        out_grad.reshape(tokens, groups, piece), "blk", split_axis=1, concat_axis=0, tiled=False
    ).reshape(groups, tokens, piece)

    slots = slot_places(expert_ids, quads, groups, capacity)
    number = jnp.arange(total, dtype=jnp.int32)[:, None]
    first = slots[:, 0][None, :] == number
    second = slots[:, 1][None, :] == number
    pick = (first | second).astype(BF16)
    scale = jnp.sum(
        jnp.where(first, combine[:, 0][None, :], 0.0)
        + jnp.where(second, combine[:, 1][None, :], 0.0),
        axis=1,
        keepdims=True,
    )
    send_x = dot(pick, layer_input, 1, 0).astype(BF16)
    send_w = (dot(pick, out_grad, 1, 0) * scale).astype(BF16)
    both = ("quad", "blk")
    rows_x = lax.all_to_all(send_x, both, split_axis=0, concat_axis=0, tiled=True)
    rows_w = lax.all_to_all(send_w, both, split_axis=0, concat_axis=0, tiled=True)
    rows_x = lax.all_gather(rows_x, "shard", tiled=True)
    rows_w = lax.all_gather(rows_w, "shard", tiled=True)

    gate_w, up_w, down_w = w_gate[0, 0], w_up[0, 0], w_down[0, 0]
    gate = dot(rows_x, gate_w, 1, 0)
    upper = dot(rows_x, up_w, 1, 0)
    sigma = jax.nn.sigmoid(gate)
    active = gate * sigma
    hidden = (active * upper).astype(BF16)
    d_hidden = dot(rows_w, down_w, 1, 1)
    d_up = (d_hidden * active).astype(BF16)
    d_gate = (d_hidden * upper * sigma * (1.0 + gate * (1.0 - sigma))).astype(BF16)
    part = (dot(d_gate, gate_w, 1, 1) + dot(d_up, up_w, 1, 1)).astype(BF16)
    grad_d = dot(hidden, rows_w, 0, 0).astype(BF16)
    grad_g = dot(rows_x, d_gate, 0, 0).astype(BF16)
    grad_u = dot(rows_x, d_up, 0, 0).astype(BF16)

    summed = lax.psum_scatter(part, "shard", scatter_dimension=0, tiled=True)
    outward = summed.reshape(quads, groups * capacity, groups, piece).transpose(0, 2, 1, 3)
    outward = outward.reshape(experts, groups * capacity, piece)
    back = lax.all_to_all(outward, both, split_axis=0, concat_axis=0, tiled=True)
    back = back.reshape(experts, groups, capacity, piece)

    embs = []
    for z in range(groups):
        places = slot_places(all_ids[z], quads, groups, capacity)
        put = (
            (places[:, 0][:, None] == number.T) | (places[:, 1][:, None] == number.T)
        ).astype(BF16)
        moved = dot(put, back[:, z].reshape(total, piece), 1, 0)
        embs.append((grad_pieces[z].astype(F32) + moved).astype(BF16))
    emb = jnp.concatenate(embs, axis=0)
    emb_all = lax.all_gather(emb, ("quad", "shard"), tiled=True)

    base = (lax.axis_index("quad") * SHARDS + lax.axis_index("shard")) * BUCK_DEV
    local = all_buckets - base
    hot = (local[:, :, None] == jnp.arange(BUCK_DEV)[None, None, :]).astype(BF16)
    hot = hot.reshape(all_buckets.shape[0], NHASH * BUCK_DEV)
    ngram = dot(hot, emb_all, 0, 0).reshape(NHASH, BUCK_DEV, piece)
    return grad_g[None, None], grad_u[None, None], grad_d[None, None], ngram


def solution(mesh):
    blocks = mesh.shape["blk"]
    quads = mesh.shape["dp"] // SHARDS
    split = Mesh(mesh.devices.reshape(quads, SHARDS, blocks), ("quad", "shard", "blk"))
    dp = ("quad", "shard")
    rows = P(dp + ("blk",), None)
    weights = P("blk", dp, None, None)
    return jax.shard_map(
        on_device,
        mesh=split,
        in_specs=(rows,) * 5 + (weights,) * 3,
        out_specs=(weights,) * 3 + (P(None, dp, "blk"),),
        check_vma=False,
    )
```

time: 535 us -> 351 us (0.66); the launches traced: 529 us -> 350 us
  local copies, waits for them, and re-layouts: 128 us -> 8.71 us
  waiting for transfers between devices: 192 us -> 116 us
  blocking collectives: 91.4 us -> 149 us
  other arithmetic: 46.9 us -> 3.99 us
  matrix products: 28.1 us -> 48.3 us
  starting transfers between devices: 27.5 us -> 9.17 us
    all_to_all x6 -> x2, waiting for transfers between devices: 164 us -> 41.3 us  [the longest x1 28.9 us: on_device(): lax.all_to_all(outward, both, split_axis=0, concat_axis=0, tiled=True)]
    all_gather x0 -> x2, blocking collectives: none -> 75.3 us  [the longest x1 64.3 us: on_device(): lax.all_gather(bucket_ids, ('quad', 'shard', 'blk'), tiled=True)]
    reshape x10 -> x2, local copies, waits for them, and re-layouts: 53 us -> 4.53 us  [on_device(): summed.reshape(quads, groups * capacity, groups, piece)]
    all_gather x0 -> x3, waiting for transfers between devices: none -> 35.3 us  [the longest x1 32.8 us: on_device(): rows_w = lax.all_gather(rows_w, 'shard', tiled=True)]
    gather x5 -> x0, local copies, waits for them, and re-layouts: 21.2 us -> none  [the longest x1 6.87 us: on_device(): bucket_flat[owner_source] % BUCK_DEV]
    dot_general x8 -> x20, matrix products: 28.1 us -> 48.3 us  [the longest x15 47.3 us: dot(): lax.dot_general(a, b, (((ca,), (cb,)), ((), ())), preferred_element_type=...]
    all_to_all x3 -> x0, local copies, waits for them, and re-layouts: 18.5 us -> none  [the longest x1 7.61 us: on_device(): lax.all_to_all(partials, 'dp', split_axis=1, concat_axis=1, tiled=True)]
    all_to_all x6 -> x2, starting transfers between devices: 27.4 us -> 9.01 us  [the longest x1 5.53 us: on_device(): lax.all_to_all(outward, both, split_axis=0, concat_axis=0, tiled=True)]
  transfers between devices with their start and end apart: 7 -> 6, of which waited for: 6 -> 5; matrix products, arithmetic and copies ran while one was open for 20% -> 8% of each run, Pallas kernels for 0% -> 0%
where the time goes in v1:
time: 351 us; the launch traced here: 350 us
  blocking collectives  149 us (42%)
  waiting for transfers between devices  116 us (33%)
  matrix products  48.3 us (14%)
  between operations  14.2 us (4%)
  starting transfers between devices  9.17 us (3%)
  local copies, waits for them, and re-layouts  8.71 us (2%)
  other arithmetic  3.99 us (1%)
    all_gather x1, blocking collectives, on_device(): lax.all_gather(bucket_ids, ('quad', 'shard', 'blk'), tiled=True)  64.3 us
    dot_general x15, matrix products, dot(): lax.dot_general(a, b, (((ca,), (cb,)), ((), ())), preferred_element_type=...  47.3 us
    reduce_scatter x1, waiting for transfers between devices, on_device(): summed = lax.psum_scatter(part, 'shard', scatter_dimension=0, tiled=True)  39.8 us
    all_to_all x1, blocking collectives, on_device(): lax.all_to_all(send_x, both, split_axis=0, concat_axis=0, tiled=True)  39.6 us
    all_to_all x1, blocking collectives, on_device(): lax.all_to_all(send_w, both, split_axis=0, concat_axis=0, tiled=True)  34.5 us
    all_gather x1, waiting for transfers between devices, on_device(): rows_w = lax.all_gather(rows_w, 'shard', tiled=True)  32.8 us
    all_to_all x1, waiting for transfers between devices, on_device(): lax.all_to_all(outward, both, split_axis=0, concat_axis=0, tiled=True)  28.9 us
    all_to_all x1, waiting for transfers between devices, on_device(): lax.all_to_all(out_grad.reshape(tokens, groups, piece), 'blk', split_axis...  12.4 us
  transfers between devices with their start and end apart: 6, of which 5 were waited for; matrix products, arithmetic and copies ran while one was open for 8% of the time, Pallas kernels for 0%

profile of v1, /device:TPU:0, one launch (start us, length us, event | category | flops | bytes accessed | tf_op | source)
XLA Modules:
  0.0 350.2 jit_solution(12893725321501455190)
XLA Ops:
  9.0 1.5 convolution_convert_fusion.3
  10.5 39.6 %all_to_all.44 = bf16[8,40,2048]{2,1,0:T(8,128)(2,1)} all-to-all(bf16[8,40,2048]{2,1,0:T(8,128)(2,1)S(1)} %bitcast.118), channel_id=1, replica_groups=mesh['quad'=2,'shard'=4,'blk'=4] {'quad','blk'}, dimensions={0} | all-to-all | bytes 2621440 | tf_op jit(solution)/shard_map/all_to_all | solution.py:57
  50.9 34.5 %all_to_all.45 = bf16[8,40,2048]{2,1,0:T(8,128)(2,1)} all-to-all(bf16[8,40,2048]{2,1,0:T(8,128)(2,1)S(1)} %bitcast.117), channel_id=1, replica_groups=mesh['quad'=2,'shard'=4,'blk'=4] {'quad','blk'}, dimensions={0} | all-to-all | bytes 2621440 | tf_op jit(solution)/shard_map/all_to_all | solution.py:58
  85.5 2.5 all-gather.5.cloned.1.call-done
  88.0 5.9 %fusion.9 = f32[1280,352]{0,1:T(8,128)} fusion(bf16[1280,2048]{1,0:T(8,128)(2,1)} %all-gather.5.cloned.1.call-done, bf16[1,1,2048,352]{2,3,1,0:T(8,128)(2,1)S(1)} %copy-done), kind=kOutput, calls=%fused_computation.20 | convolution fusion | flops 1845493760 | bytes 8486912 | tf_op jit(solution)/shard_map/dot_general | solution.py:14
  93.9 3.4 fusion.12
  97.3 32.8 %all-gather.7.cloned.1.call-done = bf16[1280,2048]{1,0:T(8,128)(2,1)} async-done(((bf16[320,2048]{1,0:T(8,128)(2,1)}), bf16[1280,2048]{1,0:T(8,128)(2,1)}) %all-gather.7.cloned.1.call-update) | async-done | bytes 5242896 | tf_op jit(solution)/shard_map/all_gather | solution.py:60
  130.1 6.4 %multiply_convert_fusion.1 = (bf16[1280,352]{0,1:T(8,128)(2,1)S(1)}, bf16[1280,352]{0,1:T(8,128)(2,1)S(1)}) fusion(f32[1280,352]{0,1:T(8,128)} %fusion.9, f32[1280,352]{0,1:T(8,128)} %fusion.12, bf16[1280,2048]{1,0:T(8,128)(2,1)} %all-gather.7.cloned.1.call-done, bf16[1,1,352,2048]{3,2,1,0:T(8,128)(2,1)} %param.15), kind=kOutput, calls=%fused_computation.14 | convolution fusion | flops 1851351040 | bytes 12091392 | tf_op jit(solution)/shard_map/dot_general | solution.py:14
  136.6 2.9 fusion.7
  139.5 4.7 %add_convert_fusion = bf16[1280,2048]{1,0:T(8,128)(2,1)} fusion(f32[1280,2048]{1,0:T(8,128)S(1)} %fusion.7, bf16[1280,352]{0,1:T(8,128)(2,1)S(1)} %get-tuple-element.4, bf16[1,1,2048,352]{2,3,1,0:T(8,128)(2,1)S(1)} %copy-done.2), kind=kOutput, calls=%fused_computation | convolution fusion | flops 1850736640 | bytes 18071552 | tf_op jit(solution)/shard_map/dot_general | solution.py:14
  144.9 11.0 %all-gather = s32[512,2]{0,1:T(2,128)S(1)} all-gather(s32[128,2]{0,1:T(2,128)S(1)} %copy-done.7), channel_id=2, replica_groups=mesh['quad'=2,'shard'=4,'blk'=4] {'blk'}, dimensions={0}, use_global_device_ids=true | all-gather | bytes 5120 | tf_op jit(solution)/shard_map/all_gather | solution.py:37
  156.0 39.8 %reduce-scatter.2.cloned.1.call-done = bf16[320,2048]{1,0:T(8,128)(2,1)} async-done(((bf16[1280,2048]{1,0:T(8,128)(2,1)}), bf16[320,2048]{1,0:T(8,128)(2,1)}) %reduce-scatter.2.cloned.1.call-update) | async-done | bytes 1310736 | tf_op jit(solution)/shard_map/reduce_scatter | solution.py:76
  195.7 3.2 reshape.255
  200.3 5.5 %all-to-all-start.3 = ((bf16[8,160,512]{2,1,0:T(8,128)(2,1)}), bf16[8,160,512]{2,1,0:T(8,128)(2,1)S(1)}, u32[]{:S(2)}, u32[]{:S(2)}) async-start(bf16[8,160,512]{2,1,0:T(8,128)(2,1)} %bitcast.114), calls=%async_computation.4 | async-start | bytes 2621440 | tf_op jit(solution)/shard_map/all_to_all | solution.py:79
  205.8 1.3 copy.48
  209.1 28.9 %all-to-all-done.3 = bf16[8,160,512]{2,1,0:T(8,128)(2,1)S(1)} async-done(((bf16[8,160,512]{2,1,0:T(8,128)(2,1)}), bf16[8,160,512]{2,1,0:T(8,128)(2,1)S(1)}, u32[]{:S(2)}, u32[]{:S(2)}) %all-to-all-start.3) | async-done | bytes 1310752 | tf_op jit(solution)/shard_map/all_to_all | solution.py:79
  238.0 3.5 all-to-all-start.2
  242.7 12.4 %all-to-all-done.2 = bf16[1,128,4,512]{3,1,0,2:T(8,128)(2,1)S(1)} async-done(((bf16[1,128,4,512]{3,1,0,2:T(8,128)(2,1)}), bf16[1,128,4,512]{3,1,0,2:T(8,128)(2,1)S(1)}, u32[]{:S(2)}, u32[]{:S(2)}) %all-to-all-start.2) | async-done | bytes 524320 | tf_op jit(solution)/shard_map/all_to_all | solution.py:39
  260.0 64.3 %all_gather.20 = s32[4096,4]{0,1:T(4,128)S(1)} all-gather(s32[128,4]{0,1:T(4,128)S(1)} %copy-done.8), channel_id=1, replica_groups=mesh['quad'=2,'shard'=4,'blk'=4] {'quad','shard','blk'}, dimensions={0}, use_global_device_ids=true | all-gather | bytes 67584 | tf_op jit(solution)/shard_map/all_gather | solution.py:38
  324.3 1.3 bitcast_compare_fusion
  325.7 6.0 %fusion.4 = bf16[1,1,2048,352]{2,3,1,0:T(8,128)(2,1)} fusion(bf16[1280,352]{0,1:T(8,128)(2,1)} %copy-done.5, bf16[1280,2048]{1,0:T(8,128)(2,1)} %all-gather.5.cloned.1.call-done), kind=kOutput, calls=%fused_computation.11 | convolution fusion | flops 1846214656 | bytes 7585792 | tf_op jit(solution)/shard_map/dot_general | solution.py:14
  331.8 3.1 fusion.5
  334.9 3.2 fusion.3
  338.2 5.5 %fusion = f32[4,128,512]{2,1,0:T(8,128)} fusion(pred[4,128,4096]{2,1,0:T(32,128)(4,1)S(1)} %bitcast.119, bf16[4096,512]{1,0:T(8,128)(2,1)} %all-gather.9.cloned.1.call-done), kind=kOutput, calls=%fused_computation.2 | convolution fusion | flops 2147483648 | bytes 7340032 | tf_op jit(solution)/shard_map/dot_general | solution.py:14
  (84 shorter events, 12.6 us)
Async XLA Ops:
  7.2 80.9 %copy-start = (bf16[1,1,2048,352]{2,3,1,0:T(8,128)(2,1)S(1)}, bf16[1,1,2048,352]{2,3,1,0:T(8,128)(2,1)}, u32[]{:S(2)}) copy-start(bf16[1,1,2048,352]{2,3,1,0:T(8,128)(2,1)} %param.13) | copy-start | bytes 4325380
  7.2 80.8 %all-gather.5.cloned.1.call-start = ((), (), s32[]{:S(2)}) async-start(), calls=%async_computation.5 | async-start | bytes 6553600 | tf_op jit(solution)/shard_map/all_gather | solution.py:59
  10.5 39.7 %copy-start.9 = (f32[128,2]{0,1:T(2,128)S(1)}, f32[128,2]{0,1:T(2,128)}, u32[]{:S(2)}) copy-start(f32[128,2]{0,1:T(2,128)} %param.11) | copy-start | bytes 3076
  10.5 39.9 %copy-start.1 = (bf16[128,2048]{1,0:T(8,128)(2,1)S(1)}, bf16[128,2048]{1,0:T(8,128)(2,1)}, u32[]{:S(2)}) copy-start(bf16[128,2048]{1,0:T(8,128)(2,1)} %param.9) | copy-start | bytes 1572868
  50.2 79.9 %all-gather.7.cloned.1.call-start = ((), (), s32[]{:S(2)}) async-start(), calls=%async_computation.6 | async-start | bytes 6553600 | tf_op jit(solution)/shard_map/all_gather | solution.py:60
  85.5 8.5 %copy-start.2 = (bf16[1,1,2048,352]{2,3,1,0:T(8,128)(2,1)S(1)}, bf16[1,1,2048,352]{2,3,1,0:T(8,128)(2,1)}, u32[]{:S(2)}) copy-start(bf16[1,1,2048,352]{2,3,1,0:T(8,128)(2,1)} %param.14) | copy-start | bytes 4325380
  85.5 110.2 %reduce-scatter.2.cloned.1.call-start = ((), (), s32[]{:S(2)}) async-start(), calls=%async_computation.7 | async-start | bytes 6553600 | tf_op jit(solution)/shard_map/reduce_scatter | solution.py:76
  88.0 5.9 %copy-start.10 = (bf16[1280,2048]{1,0:T(8,128)(2,1)S(1)}, bf16[1280,2048]{1,0:T(8,128)(2,1)}, u32[]{:S(2)}) copy-start(bf16[1280,2048]{1,0:T(8,128)(2,1)} %all-gather.5.cloned.1.call-done) | copy-start | bytes 15728644
  136.5 3.0 copy-start.5
  136.6 3.0 copy-start.3
  144.2 0.7 copy-start.7
  200.3 37.8 %all-to-all-start.3 = ((bf16[8,160,512]{2,1,0:T(8,128)(2,1)}), bf16[8,160,512]{2,1,0:T(8,128)(2,1)S(1)}, u32[]{:S(2)}, u32[]{:S(2)}) async-start(bf16[8,160,512]{2,1,0:T(8,128)(2,1)} %bitcast.114), calls=%async_computation.4 | async-start | bytes 2621440 | tf_op jit(solution)/shard_map/all_to_all | solution.py:79
  238.0 17.0 %all-to-all-start.2 = ((bf16[1,128,4,512]{3,1,0,2:T(8,128)(2,1)}), bf16[1,128,4,512]{3,1,0,2:T(8,128)(2,1)S(1)}, u32[]{:S(2)}, u32[]{:S(2)}) async-start(bf16[1,128,4,512]{3,1,0,2:T(8,128)(2,1)} %copy.49), calls=%async_computation.2 | async-start | bytes 1048576 | tf_op jit(solution)/shard_map/all_to_all | solution.py:39
  241.5 96.7 %all-gather.9.cloned.1.call-start = ((), (), s32[]{:S(2)}) async-start(), calls=%async_computation.8 | async-start | bytes 4718592 | tf_op jit(solution)/shard_map/all_gather | solution.py:91
  242.7 16.1 %copy-start.6 = (bf16[8,1,40,512]{3,2,1,0:T(8,128)(2,1)S(1)}, bf16[8,1,40,512]{3,2,1,0:T(8,128)(2,1)}, u32[]{:S(2)}) copy-start(bf16[8,1,40,512]{3,2,1,0:T(8,128)(2,1)} %get-tuple-element.6) | copy-start | bytes 983044
  256.3 3.7 %copy-start.8 = (s32[128,4]{0,1:T(4,128)S(1)}, s32[128,4]{0,1:T(4,128)}, u32[]{:S(2)}) copy-start(s32[128,4]{0,1:T(4,128)} %param.12) | copy-start | bytes 6148
  324.3 7.4 %slice-start = ((s8[5242880]{0:T(1024)(128)(4,1)}), s8[4194304]{0:T(1024)(128)(4,1)S(1)}, s32[]{:S(2)}) async-start(s8[5242880]{0:T(1024)(128)(4,1)} %bitcast.129), calls=%async_computation.9 | async-start | bytes 8388608
  325.7 6.1 %copy-start.4 = (bf16[1280,352]{0,1:T(8,128)(2,1)S(1)}, bf16[1280,352]{0,1:T(8,128)(2,1)}, u32[]{:S(2)}) copy-start(bf16[1280,352]{0,1:T(8,128)(2,1)} %copy-done.3) | copy-start | bytes 2703364
  325.7 6.1 %slice-start.1 = ((s8[5242880]{0:T(1024)(128)(4,1)}), s8[1048576]{0:T(1024)(128)(4,1)S(1)}, s32[]{:S(2)}) async-start(s8[5242880]{0:T(1024)(128)(4,1)} %bitcast.129), calls=%async_computation.10 | async-start | bytes 2097152
  325.7 9.2 %slice-start.2 = ((s8[5242880]{0:T(1024)(128)(4,1)}), s8[4194304]{0:T(1024)(128)(4,1)S(1)}, s32[]{:S(2)}) async-start(s8[5242880]{0:T(1024)(128)(4,1)} %bitcast.131), calls=%async_computation.11 | async-start | bytes 8388608
  331.7 3.2 slice-start.3
  331.8 3.2 copy-start.11
  331.8 3.1 copy-start.12
Sparse Core Ops, SparseCore 0:
  50.3 37.6 all-gather.4
  89.6 40.4 all-gather.6
  144.3 51.3 reduce-scatter.1
  260.1 34.0 all-gather.8

commit v2 on v1

v2 whole, which is shorter than its diff:
```python
import functools

import jax
import jax.numpy as jnp
from jax import lax
from jax.experimental import pallas as pl
from jax.experimental.pallas import tpu as pltpu
from jax.sharding import Mesh, PartitionSpec as P

NHASH = 4
SHARDS = 4
BUCK_DEV = 128
F32 = jnp.float32
BF16 = jnp.bfloat16


def dot(a, b, ca, cb):
    return lax.dot_general(a, b, (((ca,), (cb,)), ((), ())), preferred_element_type=F32)


def slot_places(ids, quads, groups, capacity):
    tokens = ids.shape[0]
    expert_count = quads * groups
    dest = (ids % quads) * groups + ids // quads
    hot = (dest[:, :, None] == jnp.arange(expert_count)[None, None, :]).astype(F32)
    per_token = hot.sum(axis=1)
    before = jnp.tril(jnp.ones((tokens, tokens), F32), -1) @ per_token
    position = (hot * before[:, None, :]).sum(axis=2).astype(jnp.int32)
    return dest * capacity + position


MESH = pl.DeviceIdType.MESH
SHARD = ("half", "core")


def place():
    return tuple(lax.axis_index(name) for name in ("quad", "half", "core", "blk"))


def greet(partners):
    barrier = pltpu.get_barrier_semaphore()
    for partner in partners:
        pl.semaphore_signal(barrier, inc=1, device_id=partner, device_id_type=MESH)
    pl.semaphore_wait(barrier, len(partners))


def remote(src, dst, sends, recvs, index, partner):
    return pltpu.make_async_remote_copy(
        src_ref=src,
        dst_ref=dst,
        send_sem=sends.at[index],
        recv_sem=recvs.at[index],
        device_id=partner,
        device_id_type=MESH,
    )


def return_kernel(
    quads, groups, part, grad, out, pieces, near, pair_sum, far, full, own_sem,
    sends1, recvs1, sends2, recvs2, sends3, recvs3, sends4, recvs4,
):
    q, x, c, z = place()
    rows, piece = full.shape[1], full.shape[2]
    quarter_rows = rows // quads
    others = [(k, j) for k in list(range(1, groups)) + [0] for j in range(quads) if k or j]
    order = list(range(1, groups)) + [0]

    def seat(k, j):
        return (lax.rem(q + j, quads), x, c, lax.rem(z + k, groups))

    other_core = (q, x, 1 - c, z)
    other_half = (q, 1 - x, c, z)
    greet([other_core, other_half] + [seat(k, j) for k, j in others])

    def block(k, j, core):
        half = lax.rem(x + 1 + j, 2)
        row = pl.multiple_of((half * 2 + core) * rows, 32)
        col = pl.multiple_of(lax.rem(z + k, groups) * piece, 128)
        return row, col

    def first(k, j):
        row, col = block(k, j, 1 - c)
        return remote(
            part.at[pl.ds(row, rows), pl.ds(col, piece)], near.at[j, k],
            sends1, recvs1, j * groups + k, other_core,
        )

    def second(k):
        return remote(pair_sum.at[k], far.at[k], sends2, recvs2, k, other_half)

    def third(k, j):
        start = pl.multiple_of(lax.rem(q + j, quads) * quarter_rows, 16)
        return remote(
            full.at[k, pl.ds(start, quarter_rows)], out.at[q * groups + z],
            sends3, recvs3, k * quads + j, seat(k, j),
        )

    def fourth(k):
        col = pl.multiple_of(lax.rem(z + k, groups) * piece, 128)
        return remote(
            grad.at[:, pl.ds(col, piece)], pieces.at[z], sends4, recvs4, k, seat(k, 0)
        )

    for j in range(2):
        for k in order:
            first(k, j).start()
    for k in range(1, groups):
        fourth(k).start()
    own_grad = pltpu.make_async_copy(
        grad.at[:, pl.ds(pl.multiple_of(z * piece, 128), piece)], pieces.at[z], own_sem.at[0]
    )
    own_grad.start()

    step = 32
    for k in order:
        first(k, 0).wait_recv()
        row, col = block(k, 0, c)

        @pl.loop(0, rows // step)
        def _(i):
            at = pl.multiple_of(i * step, step)
            mine = part[pl.ds(pl.multiple_of(row + at, step), step), pl.ds(col, piece)]
            theirs = near[0, k, pl.ds(at, step), :]
            pair_sum[k, pl.ds(at, step), :] = (mine.astype(F32) + theirs.astype(F32)).astype(BF16)

        second(k).start()
    for k in order:
        first(k, 1).wait_recv()
        second(k).wait_recv()
        row, col = block(k, 1, c)

        @pl.loop(0, rows // step)
        def _(i):
            at = pl.multiple_of(i * step, step)
            mine = part[pl.ds(pl.multiple_of(row + at, step), step), pl.ds(col, piece)]
            total = mine.astype(F32) + near[1, k, pl.ds(at, step), :].astype(F32)
            total = total + far[k, pl.ds(at, step), :].astype(F32)
            full[k, pl.ds(at, step), :] = total.astype(BF16)

        for j in range(quads):
            if k or j:
                third(k, j).start()
    kept = pltpu.make_async_copy(
        full.at[0, pl.ds(pl.multiple_of(q * quarter_rows, 16), quarter_rows)],
        out.at[q * groups + z],
        own_sem.at[1],
    )
    kept.start()

    def third_in(k, j):
        source = lax.rem(q + quads - j, quads) * groups + lax.rem(z + groups - k, groups)
        return remote(
            full.at[k, pl.ds(0, quarter_rows)], out.at[source],
            sends3, recvs3, k * quads + j, seat(k, j),
        )

    def fourth_in(k):
        return remote(
            grad.at[:, pl.ds(0, piece)], pieces.at[lax.rem(z + groups - k, groups)],
            sends4, recvs4, k, seat(k, 0),
        )

    own_grad.wait()
    for k in range(1, groups):
        fourth(k).wait_send()
        fourth_in(k).wait_recv()
    for k in order:
        first(k, 0).wait_send()
        first(k, 1).wait_send()
        second(k).wait_send()
    for k, j in others:
        third(k, j).wait_send()
        third_in(k, j).wait_recv()
    kept.wait()


def return_rows(part, grad, quads, groups):
    tokens, width = grad.shape
    piece = width // groups
    rows = part.shape[0] // SHARDS
    dma = pltpu.SemaphoreType.DMA
    return pl.pallas_call(
        functools.partial(return_kernel, quads, groups),
        out_shape=(
            jax.ShapeDtypeStruct((quads * groups, rows // quads, piece), BF16),
            jax.ShapeDtypeStruct((groups, tokens, piece), BF16),
        ),
        in_specs=[pl.BlockSpec(memory_space=pltpu.VMEM)] * 2,
        out_specs=[pl.BlockSpec(memory_space=pltpu.VMEM)] * 2,
        scratch_shapes=[
            pltpu.VMEM((2, groups, rows, piece), BF16),
            pltpu.VMEM((groups, rows, piece), BF16),
            pltpu.VMEM((groups, rows, piece), BF16),
            pltpu.VMEM((groups, rows, piece), BF16),
            dma((2,)),
            dma((2 * groups,)),
            dma((2 * groups,)),
            dma((groups,)),
            dma((groups,)),
            dma((groups * quads,)),
            dma((groups * quads,)),
            dma((groups,)),
            dma((groups,)),
        ],
        compiler_params=pltpu.CompilerParams(
            collective_id=0, has_side_effects=True, vmem_limit_bytes=40 << 20
        ),
        name="return_rows",
    )(part, grad)


def gather_kernel(quads, emb, out, own_sem, sends, recvs, core_sends, core_recvs):
    q, x, c, z = place()
    tokens = emb.shape[0]
    cut = tokens // 2
    other_core = (q, x, 1 - c, z)
    other_half = (q, 1 - x, c, z)

    def quad(j):
        return (lax.rem(q + j, quads), x, c, z)

    def source(j):
        return lax.rem(q + quads - j, quads)

    def seat(row, half, core):
        return row * SHARDS + half * 2 + core

    greet([other_core, other_half] + [quad(j) for j in range(1, quads)])
    mine = out.at[seat(q, x, c)]
    own = pltpu.make_async_copy(emb, mine, own_sem)
    own.start()
    low, high = pl.ds(0, cut), pl.ds(cut, cut)

    def across(src, dst, index, partner):
        return remote(src, dst, sends, recvs, index, partner)

    def core_pass(block, core_block, index):
        out_copy = remote(block, block, core_sends, core_recvs, index, other_core)
        in_copy = remote(core_block, core_block, core_sends, core_recvs, index, other_core)
        return out_copy, in_copy

    started, arriving = [], []

    def go(copy):
        copy.start()
        started.append(copy)

    def pass_on(row, half, span, index):
        here, there = out.at[seat(row, half, c)], out.at[seat(row, half, 1 - c)]
        if span is not None:
            here, there = here.at[span], there.at[span]
        out_copy, in_copy = core_pass(here, there, index)
        go(out_copy)
        arriving.append(in_copy)

    go(across(emb, mine, 0, other_half))
    for j in range(1, quads):
        go(across(emb, mine, 3 * j, quad(j)))
    go(remote(emb, mine, core_sends, core_recvs, 0, other_core))
    theirs = out.at[seat(q, x, 1 - c)]
    arriving.append(remote(theirs, theirs, core_sends, core_recvs, 0, other_core))

    half_block = out.at[seat(q, 1 - x, c)]
    across(half_block, half_block, 0, other_half).wait_recv()
    for j in range(1, quads):
        go(across(half_block.at[low], half_block.at[low], 3 * j + 1, quad(j)))
    for j in range(1, quads):
        block = out.at[seat(source(j), x, c)]
        across(block, block, 3 * j, quad(j)).wait_recv()
        go(across(block.at[high], block.at[high], 3 * j + 2, other_half))
        pass_on(source(j), x, None, 4 * j)
    pass_on(q, 1 - x, None, 1)
    for j in range(1, quads):
        block = out.at[seat(source(j), 1 - x, c)]
        across(block.at[low], block.at[low], 3 * j + 1, quad(j)).wait_recv()
        pass_on(source(j), 1 - x, low, 4 * j + 1)
        across(block.at[high], block.at[high], 3 * j + 2, other_half).wait_recv()
        pass_on(source(j), 1 - x, high, 4 * j + 2)
    own.wait()
    for copy in started:
        copy.wait_send()
    for copy in arriving:
        copy.wait_recv()


def gather_plane(emb, quads):
    tokens, piece = emb.shape
    dma = pltpu.SemaphoreType.DMA
    return pl.pallas_call(
        functools.partial(gather_kernel, quads),
        out_shape=jax.ShapeDtypeStruct((quads * SHARDS, tokens, piece), BF16),
        in_specs=[pl.BlockSpec(memory_space=pltpu.VMEM)],
        out_specs=pl.BlockSpec(memory_space=pltpu.VMEM),
        scratch_shapes=[
            dma,
            dma((3 * quads,)),
            dma((3 * quads,)),
            dma((4 * quads,)),
            dma((4 * quads,)),
        ],
        compiler_params=pltpu.CompilerParams(
            collective_id=1, has_side_effects=True, vmem_limit_bytes=40 << 20
        ),
        name="gather_plane",
    )(emb)


def on_device(layer_input, out_grad, expert_ids, combine, bucket_ids, w_gate, w_up, w_down):
    groups = lax.axis_size("blk")
    quads = lax.axis_size("quad")
    experts = groups * quads
    tokens, width = layer_input.shape
    capacity = 5 * tokens // (2 * experts)
    piece = width // groups
    while groups * capacity % 16:
        capacity += 1
    total = experts * capacity

    keys = jnp.concatenate([bucket_ids, expert_ids], axis=1)
    all_keys = lax.all_gather(keys, ("quad", "half", "core", "blk"), tiled=True)
    all_buckets = all_keys[:, :NHASH]
    seat = (lax.axis_index("quad") * 2 + lax.axis_index("half")) * 2 + lax.axis_index("core")
    column = lax.dynamic_slice_in_dim(
        all_keys[:, NHASH:], seat * groups * tokens, groups * tokens, 0
    ).reshape(groups, tokens, 2)

    slots = slot_places(expert_ids, quads, groups, capacity)
    number = jnp.arange(total, dtype=jnp.int32)[:, None]
    first = slots[:, 0][None, :] == number
    second = slots[:, 1][None, :] == number
    pick = (first | second).astype(BF16)
    scale = jnp.sum(
        jnp.where(first, combine[:, 0][None, :], 0.0)
        + jnp.where(second, combine[:, 1][None, :], 0.0),
        axis=1,
        keepdims=True,
    )
    send_x = dot(pick, layer_input, 1, 0).astype(BF16)
    send_w = (dot(pick, out_grad, 1, 0) * scale).astype(BF16)
    both = ("quad", "blk")
    rows_x = lax.all_to_all(send_x, both, split_axis=0, concat_axis=0, tiled=True)
    rows_w = lax.all_to_all(send_w, both, split_axis=0, concat_axis=0, tiled=True)
    rows_x = lax.all_gather(rows_x, SHARD, tiled=True)
    rows_w = lax.all_gather(rows_w, SHARD, tiled=True)

    gate_w, up_w, down_w = w_gate[0, 0], w_up[0, 0], w_down[0, 0]
    gate = dot(rows_x, gate_w, 1, 0)
    upper = dot(rows_x, up_w, 1, 0)
    sigma = jax.nn.sigmoid(gate)
    active = gate * sigma
    hidden = (active * upper).astype(BF16)
    d_hidden = dot(rows_w, down_w, 1, 1)
    d_up = (d_hidden * active).astype(BF16)
    d_gate = (d_hidden * upper * sigma * (1.0 + gate * (1.0 - sigma))).astype(BF16)
    part = (dot(d_gate, gate_w, 1, 1) + dot(d_up, up_w, 1, 1)).astype(BF16)
    grad_d = dot(hidden, rows_w, 0, 0).astype(BF16)
    grad_g = dot(rows_x, d_gate, 0, 0).astype(BF16)
    grad_u = dot(rows_x, d_up, 0, 0).astype(BF16)

    back, grad_pieces = return_rows(part, out_grad, quads, groups)
    puts = []
    for z in range(groups):
        places = slot_places(column[z], quads, groups, capacity)
        expert, position = places // capacity, places % capacity
        puts.append((expert * groups + z) * capacity + position)
    puts = jnp.concatenate(puts, axis=0)
    slot_number = jnp.arange(groups * total, dtype=jnp.int32)[None, :]
    put = (puts[:, :1] == slot_number) | (puts[:, 1:] == slot_number)
    moved = dot(put.astype(BF16), back.reshape(groups * total, piece), 1, 0)
    emb = (grad_pieces.reshape(groups * tokens, piece).astype(F32) + moved).astype(BF16)
    emb_all = gather_plane(emb, quads).reshape(-1, piece)

    base = seat * BUCK_DEV
    local = all_buckets - base
    hot = (local[:, :, None] == jnp.arange(BUCK_DEV)[None, None, :]).astype(BF16)
    hot = hot.reshape(all_buckets.shape[0], NHASH * BUCK_DEV)
    ngram = dot(hot, emb_all, 0, 0).reshape(NHASH, BUCK_DEV, piece)
    return grad_g[None, None], grad_u[None, None], grad_d[None, None], ngram


def solution(mesh):
    blocks = mesh.shape["blk"]
    quads = mesh.shape["dp"] // SHARDS
    split = Mesh(mesh.devices.reshape(quads, 2, 2, blocks), ("quad", "half", "core", "blk"))
    dp = ("quad",) + SHARD
    rows = P(dp + ("blk",), None)
    weights = P("blk", dp, None, None)
    return jax.shard_map(
        on_device,
        mesh=split,
        in_specs=(rows,) * 5 + (weights,) * 3,
        out_specs=(weights,) * 3 + (P(None, dp, "blk"),),
        check_vma=False,
    )
```

time: 351 us -> 265 us (0.75)
  waiting for transfers between devices: 116 us -> 0.06 us
  Pallas kernels: 0 us -> 67.4 us
  blocking collectives: 149 us -> 139 us
  matrix products: 48.3 us -> 38.8 us
  starting transfers between devices: 9.17 us -> 0.08 us
  local copies, waits for them, and re-layouts: 8.71 us -> 0.12 us
    pallas_call x0 -> x2, Pallas kernels: none -> 67.4 us  [the longest x1 41.9 us: return_rows(): pl.pallas_call(functools.partial(return_kernel, quads, groups), out_shape...]
    all_to_all x2 -> x0, waiting for transfers between devices: 41.3 us -> none  [the longest x1 28.9 us: on_device(): lax.all_to_all(outward, both, split_axis=0, concat_axis=0, tiled=True)]
    reduce_scatter x1 -> x0, waiting for transfers between devices: 39.8 us -> none  [on_device(): summed = lax.psum_scatter(part, 'shard', scatter_dimension=0, tiled=True)]
    all_gather x3 -> x2, waiting for transfers between devices: 35.3 us -> 0.02 us  [the longest x1 0.02 us: on_device(): rows_x = lax.all_gather(rows_x, SHARD, tiled=True)]
    all_gather x2 -> x1, blocking collectives: 75.3 us -> 65.1 us  [on_device(): all_keys = lax.all_gather(keys, ('quad', 'half', 'core', 'blk'), tiled=True)]
    dot_general x15 -> x12, matrix products: 47.3 us -> 37.8 us  [dot(): lax.dot_general(a, b, (((ca,), (cb,)), ((), ())), preferred_element_type=...]
    all_to_all x2 -> x0, starting transfers between devices: 9.01 us -> none  [the longest x1 5.53 us: on_device(): lax.all_to_all(outward, both, split_axis=0, concat_axis=0, tiled=True)]
    reshape x2 -> x0, local copies, waits for them, and re-layouts: 4.53 us -> none  [on_device(): summed.reshape(quads, groups * capacity, groups, piece)]
  transfers between devices with their start and end apart: 6 -> 2, of which waited for: 5 -> 0; matrix products, arithmetic and copies ran while one was open for 8% -> 5% of each run, Pallas kernels for 0% -> 0%
where the time goes in v2:
time: 265 us; the launch traced here: 264 us
  blocking collectives  139 us (52%)
  Pallas kernels  67.4 us (25%)
  matrix products  38.8 us (15%)
  between operations  14.4 us (5%)
  other arithmetic  4.21 us (2%)
    all_gather x1, blocking collectives, on_device(): all_keys = lax.all_gather(keys, ('quad', 'half', 'core', 'blk'), tiled=True)  65.1 us
    pallas_call x1, Pallas kernels, return_rows(): pl.pallas_call(functools.partial(return_kernel, quads, groups), out_shape...  41.9 us
    all_to_all x1, blocking collectives, on_device(): lax.all_to_all(send_x, both, split_axis=0, concat_axis=0, tiled=True)  39.6 us
    dot_general x12, matrix products, dot(): lax.dot_general(a, b, (((ca,), (cb,)), ((), ())), preferred_element_type=...  37.8 us
    all_to_all x1, blocking collectives, on_device(): lax.all_to_all(send_w, both, split_axis=0, concat_axis=0, tiled=True)  34.5 us
    pallas_call x1, Pallas kernels, gather_plane(): pl.pallas_call(functools.partial(gather_kernel, quads), out_shape=jax.Sha...  25.5 us
  transfers between devices with their start and end apart: 2, of which 0 were waited for; matrix products, arithmetic and copies ran while one was open for 5% of the time, Pallas kernels for 0%

profile of v2, /device:TPU:0, one launch (start us, length us, event | category | flops | bytes accessed | tf_op | source)
XLA Modules:
  0.0 264.3 jit_solution(918202104537125334)
XLA Ops:
  7.2 0.8 fusion.59
  8.0 0.2 fusion.35
  8.3 0.7 convert_add_fusion
  9.0 1.5 convolution_convert_fusion.3
  10.5 39.6 %all_to_all.24 = bf16[8,40,2048]{2,1,0:T(8,128)(2,1)} all-to-all(bf16[8,40,2048]{2,1,0:T(8,128)(2,1)S(1)} %bitcast.74), channel_id=1, replica_groups=mesh['quad'=2,'half'=2,'core'=2,'blk'=4] {'quad','blk'}, dimensions={0} | all-to-all | bytes 2621440 | tf_op jit(solution)/shard_map/all_to_all | solution.py:341
  50.4 0.5 fusion
  50.9 34.5 %all_to_all.25 = bf16[8,40,2048]{2,1,0:T(8,128)(2,1)} all-to-all(bf16[8,40,2048]{2,1,0:T(8,128)(2,1)S(1)} %bitcast.73), channel_id=1, replica_groups=mesh['quad'=2,'half'=2,'core'=2,'blk'=4] {'quad','blk'}, dimensions={0} | all-to-all | bytes 2621440 | tf_op jit(solution)/shard_map/all_to_all | solution.py:342
  85.5 65.1 %all_gather.11 = s32[4096,6]{0,1:T(8,128)S(1)} all-gather(s32[128,6]{0,1:T(8,128)S(1)} %pad_add_fusion), channel_id=1, replica_groups=mesh['quad'=2,'half'=2,'core'=2,'blk'=4] {'quad','half','core','blk'}, dimensions={0}, use_global_device_ids=true | all-gather | bytes 101376 | tf_op jit(solution)/shard_map/all_gather | solution.py:320
  150.6 2.3 bitcast_compare_fusion
  153.2 0.2 fusion.29
  153.5 0.2 fusion.31
  153.7 0.2 fusion.27
  154.1 5.9 %fusion.10 = f32[1280,352]{0,1:T(8,128)} fusion(bf16[1280,2048]{1,0:T(8,128)(2,1)} %all-gather.3.cloned.1.call-done, bf16[1,1,2048,352]{2,3,1,0:T(8,128)(2,1)S(1)} %copy-done), kind=kOutput, calls=%fused_computation.22 | convolution fusion | flops 1845493760 | bytes 8486912 | tf_op jit(solution)/shard_map/dot_general | solution.py:18
  160.1 3.3 %fusion.13 = f32[1280,352]{0,1:T(8,128)} fusion(bf16[1280,2048]{1,0:T(8,128)(2,1)S(1)} %copy-done.7, bf16[1,1,2048,352]{2,3,1,0:T(8,128)(2,1)S(1)} %copy-done.3), kind=kOutput, calls=%fused_computation.25 | convolution fusion | flops 1845493760 | bytes 8486912 | tf_op jit(solution)/shard_map/dot_general | solution.py:18
  163.4 6.4 %multiply_convert_fusion.1 = (bf16[1280,352]{0,1:T(8,128)(2,1)S(1)}, bf16[1280,352]{0,1:T(8,128)(2,1)S(1)}) fusion(f32[1280,352]{0,1:T(8,128)} %fusion.10, f32[1280,352]{0,1:T(8,128)} %fusion.13, bf16[1280,2048]{1,0:T(8,128)(2,1)} %all-gather.5.cloned.1.call-done, bf16[1,1,352,2048]{3,2,1,0:T(8,128)(2,1)} %param.15), kind=kOutput, calls=%fused_computation.16 | convolution fusion | flops 1851351040 | bytes 12091392 | tf_op jit(solution)/shard_map/dot_general | solution.py:18
  169.8 2.9 %fusion.8 = f32[1280,2048]{1,0:T(8,128)S(1)} fusion(bf16[1280,352]{0,1:T(8,128)(2,1)S(1)} %get-tuple-element.9, bf16[1,1,2048,352]{2,3,1,0:T(8,128)(2,1)S(1)} %copy-done), kind=kOutput, calls=%fused_computation.20 | convolution fusion | flops 1845493760 | bytes 12828672 | tf_op jit(solution)/shard_map/dot_general | solution.py:18
  172.8 3.3 %add_convert_fusion.part = bf16[1280,2048]{1,0:T(8,128)(2,1)S(1)} fusion(f32[1280,2048]{1,0:T(8,128)S(1)} %fusion.8, bf16[1280,352]{0,1:T(8,128)(2,1)S(1)} %get-tuple-element.8, bf16[1,1,2048,352]{2,3,1,0:T(8,128)(2,1)S(1)} %copy-done.3), kind=kOutput, calls=%fused_computation | convolution fusion | flops 1850736640 | bytes 18071552 | tf_op jit(solution)/shard_map/dot_general | solution.py:18
  176.1 41.9 %return_rows.1 = (bf16[8,160,512]{2,1,0:T(8,128)(2,1)S(1)}, bf16[4,128,512]{2,1,0:T(8,128)(2,1)S(1)}) custom-call(bf16[1280,2048]{1,0:T(8,128)(2,1)S(1)} %add_convert_fusion.part, bf16[128,2048]{1,0:T(8,128)(2,1)S(1)} %copy-done.1), custom_call_target="tpu_custom_call" | custom-call | tf_op jit(solution)/shard_map/return_rows/pallas_call | solution.py:182
  217.9 0.9 fusion.22.emb
  218.9 25.5 %gather_plane.1 = bf16[8,512,512]{2,1,0:T(8,128)(2,1)S(1)} custom-call(bf16[512,512]{1,0:T(8,128)(2,1)S(1)} %fusion.22.emb), custom_call_target="tpu_custom_call" | custom-call | tf_op jit(solution)/shard_map/gather_plane/pallas_call | solution.py:289
  244.4 3.3 %fusion.84 = f32[4,128,512]{2,1,0:T(8,128)} fusion(pred[4,128,4096]{2,1,0:T(32,128)(4,1)S(1)} %bitcast.75, bf16[4096,512,1]{1,0,2:T(8,128)(2,1)S(1)} %bitcast.68), kind=kOutput, calls=%fused_computation.151 | convolution fusion | flops 2147483648 | bytes 7340032 | tf_op jit(solution)/shard_map/dot_general | solution.py:18
  247.8 3.3 %fusion.4 = bf16[1,1,352,2048]{3,2,1,0:T(8,128)(2,1)} fusion(bf16[1280,2048]{1,0:T(8,128)(2,1)S(1)} %bitcast.81, f32[1280,352]{0,1:T(8,128)S(1)} %copy-done.9, f32[1280,352]{0,1:T(8,128)S(1)} %copy-done.8), kind=kOutput, calls=%fused_computation.12 | convolution fusion | flops 1848918016 | bytes 10289152 | tf_op jit(solution)/shard_map/dot_general | solution.py:18
  251.1 3.2 %fusion.6 = bf16[1,1,2048,352]{2,3,1,0:T(8,128)(2,1)} fusion(bf16[1280,352]{0,1:T(8,128)(2,1)S(1)} %get-tuple-element.8, bf16[1280,2048]{1,0:T(8,128)(2,1)S(1)} %bitcast.79), kind=kOutput, calls=%fused_computation.14 | convolution fusion | flops 1846214656 | bytes 7585792 | tf_op jit(solution)/shard_map/dot_general | solution.py:18
  254.3 3.2 %fusion.5 = bf16[1,1,2048,352]{2,3,1,0:T(8,128)(2,1)} fusion(bf16[1280,352]{0,1:T(8,128)(2,1)S(1)} %get-tuple-element.9, bf16[1280,2048]{1,0:T(8,128)(2,1)S(1)} %bitcast.79), kind=kOutput, calls=%fused_computation.13 | convolution fusion | flops 1846214656 | bytes 7585792 | tf_op jit(solution)/shard_map/dot_general | solution.py:18
  (60 shorter events, 0.9 us)
Async XLA Ops:
  7.2 146.9 %copy-start = (bf16[1,1,2048,352]{2,3,1,0:T(8,128)(2,1)S(1)}, bf16[1,1,2048,352]{2,3,1,0:T(8,128)(2,1)}, u32[]{:S(2)}) copy-start(bf16[1,1,2048,352]{2,3,1,0:T(8,128)(2,1)} %param.13) | copy-start | bytes 4325380
  7.2 146.9 %all-gather.3.cloned.1.call-start = ((), (), s32[]{:S(2)}) async-start(), calls=%async_computation.2 | async-start | bytes 6553600 | tf_op jit(solution)/shard_map/all_gather | solution.py:343
  10.5 39.7 %copy-start.6 = (f32[128,2]{0,1:T(2,128)S(1)}, f32[128,2]{0,1:T(2,128)}, u32[]{:S(2)}) copy-start(f32[128,2]{0,1:T(2,128)} %param.11) | copy-start | bytes 3076
  10.5 39.9 %copy-start.1 = (bf16[128,2048]{1,0:T(8,128)(2,1)S(1)}, bf16[128,2048]{1,0:T(8,128)(2,1)}, u32[]{:S(2)}) copy-start(bf16[128,2048]{1,0:T(8,128)(2,1)} %grad.1) | copy-start | bytes 1572868
  50.2 113.2 %all-gather.5.cloned.1.call-start = ((), (), s32[]{:S(2)}) async-start(), calls=%async_computation.3 | async-start | bytes 6553600 | tf_op jit(solution)/shard_map/all_gather | solution.py:344
  50.9 34.6 %copy-start.4 = (s32[128,2]{0,1:T(2,128)S(1)}, s32[128,2]{0,1:T(2,128)}, u32[]{:S(2)}) copy-start(s32[128,2]{0,1:T(2,128)} %param.10) | copy-start | bytes 3076
  50.9 34.6 %copy-start.5 = (s32[128,4]{0,1:T(4,128)S(1)}, s32[128,4]{0,1:T(4,128)}, u32[]{:S(2)}) copy-start(s32[128,4]{0,1:T(4,128)} %param.12) | copy-start | bytes 6148
  154.0 6.0 %copy-start.3 = (bf16[1,1,2048,352]{2,3,1,0:T(8,128)(2,1)S(1)}, bf16[1,1,2048,352]{2,3,1,0:T(8,128)(2,1)}, u32[]{:S(2)}) copy-start(bf16[1,1,2048,352]{2,3,1,0:T(8,128)(2,1)} %param.14) | copy-start | bytes 4325380
  154.1 6.0 %copy-start.7 = (bf16[1280,2048]{1,0:T(8,128)(2,1)S(1)}, bf16[1280,2048]{1,0:T(8,128)(2,1)}, u32[]{:S(2)}) copy-start(bf16[1280,2048]{1,0:T(8,128)(2,1)} %all-gather.3.cloned.1.call-done) | copy-start | bytes 15728644
  218.8 25.6 %copy-start.2 = (pred[4096,512]{0,1:T(32,128)(4,1)S(1)}, pred[4096,512]{0,1:T(32,128)(4,1)}, u32[]{:S(2)}) copy-start(pred[4096,512]{0,1:T(32,128)(4,1)} %bitcast_compare_fusion) | copy-start | bytes 6291460
  218.9 28.9 %slice-start.2 = ((s8[5242880]{0:T(1024)(128)(4,1)}), s8[4194304]{0:T(1024)(128)(4,1)S(1)}, s32[]{:S(2)}) async-start(s8[5242880]{0:T(1024)(128)(4,1)} %bitcast.80), calls=%async_computation.6 | async-start | bytes 8388608
  244.4 3.4 %slice-start.3 = ((s8[5242880]{0:T(1024)(128)(4,1)}), s8[1048576]{0:T(1024)(128)(4,1)S(1)}, s32[]{:S(2)}) async-start(s8[5242880]{0:T(1024)(128)(4,1)} %bitcast.80), calls=%async_computation.7 | async-start | bytes 2097152
  244.4 3.3 %copy-start.8 = (f32[1280,352]{0,1:T(8,128)S(1)}, f32[1280,352]{0,1:T(8,128)}, u32[]{:S(2)}) copy-start(f32[1280,352]{0,1:T(8,128)} %fusion.10) | copy-start | bytes 5406724
  244.4 3.3 %copy-start.9 = (f32[1280,352]{0,1:T(8,128)S(1)}, f32[1280,352]{0,1:T(8,128)}, u32[]{:S(2)}) copy-start(f32[1280,352]{0,1:T(8,128)} %fusion.13) | copy-start | bytes 5406724
  244.4 6.7 %slice-start = ((s8[5242880]{0:T(1024)(128)(4,1)}), s8[1048576]{0:T(1024)(128)(4,1)S(1)}, s32[]{:S(2)}) async-start(s8[5242880]{0:T(1024)(128)(4,1)} %bitcast.78), calls=%async_computation.4 | async-start | bytes 2097152
  247.8 3.3 %slice-start.1 = ((s8[5242880]{0:T(1024)(128)(4,1)}), s8[4194304]{0:T(1024)(128)(4,1)S(1)}, s32[]{:S(2)}) async-start(s8[5242880]{0:T(1024)(128)(4,1)} %bitcast.78), calls=%async_computation.5 | async-start | bytes 8388608
Sparse Core Ops, SparseCore 0:
  50.3 37.6 all-gather.2
  89.6 40.7 all-gather.4

commit v3 on v2

--- a/solution.py
+++ b/solution.py
@@ -305,6 +305,93 @@
     )(emb)
 
 
+def dispatch_kernel(
+    quads, groups, send, out, own_sem, sends1, recvs1, sends2, recvs2, sends3, recvs3
+):
+    q, x, c, z = place()
+    count = quads * groups
+    near = [0] + sorted(range(1, groups), key=lambda k: min(k, groups - k))
+    others = [(k, j) for k in near for j in range(quads) if k or j]
+    other_core = (q, x, 1 - c, z)
+    other_half = (q, 1 - x, c, z)
+    shard = 2 * x + c
+    far_shard = 2 * (1 - x) + c
+
+    def seat(k, j):
+        return (lax.rem(q + j, quads), x, c, lax.rem(z + k, groups))
+
+    def target(k, j):
+        return lax.rem(q + j, quads) * groups + lax.rem(z + k, groups)
+
+    def source(k, j):
+        return lax.rem(q + quads - j, quads) * groups + lax.rem(z + groups - k, groups)
+
+    greet([other_core, other_half] + [seat(k, j) for k, j in others])
+    started, arriving = [], []
+
+    def go(copy):
+        copy.start()
+        started.append(copy)
+
+    def to_half(src, k, j):
+        go(remote(src, out.at[shard, source(k, j)], sends2, recvs2, k * quads + j, other_half))
+
+    def to_core(src, whose, k, j):
+        index = whose * count + k * quads + j
+        block = shard if whose == 0 else far_shard
+        go(remote(src, out.at[block, source(k, j)], sends3, recvs3, index, other_core))
+        theirs = 2 * (x if whose == 0 else 1 - x) + 1 - c
+        got = out.at[theirs, source(k, j)]
+        arriving.append(remote(got, got, sends3, recvs3, index, other_core))
+
+    def settle(k, j):
+        block = out.at[far_shard, source(k, j)]
+        remote(block, block, sends2, recvs2, k * quads + j, other_half).wait_recv()
+        to_core(block, 1, k, j)
+
+    home = q * groups + z
+    mine = send.at[home]
+    to_half(mine, 0, 0)
+    for k, j in others:
+        go(remote(
+            send.at[target(k, j)], out.at[shard, home],
+            sends1, recvs1, k * quads + j, seat(k, j),
+        ))
+    to_core(mine, 0, 0, 0)
+    own = pltpu.make_async_copy(mine, out.at[shard, home], own_sem)
+    own.start()
+    pending = [(0, 0)]
+    for k, j in others:
+        block = out.at[shard, source(k, j)]
+        remote(block, block, sends1, recvs1, k * quads + j, seat(k, j)).wait_recv()
+        to_half(block, k, j)
+        to_core(block, 0, k, j)
+        pending.append((k, j))
+        if len(pending) > 2:
+            settle(*pending.pop(0))
+    for k, j in pending:
+        settle(k, j)
+    own.wait()
+    for copy in started:
+        copy.wait_send()
+    for copy in arriving:
+        copy.wait_recv()
+
+
+def dispatch(send, quads, groups):
+    count = quads * groups
+    dma = pltpu.SemaphoreType.DMA
+    return pl.pallas_call(
+        functools.partial(dispatch_kernel, quads, groups),
+        out_shape=jax.ShapeDtypeStruct((SHARDS,) + send.shape, BF16),
+        in_specs=[pl.BlockSpec(memory_space=pl.ANY)],
+        out_specs=pl.BlockSpec(memory_space=pl.ANY),
+        scratch_shapes=[dma] + [dma((count,))] * 4 + [dma((2 * count,))] * 2,
+        compiler_params=pltpu.CompilerParams(collective_id=2, has_side_effects=True),
+        name="dispatch",
+    )(send)
+
+
 def on_device(layer_input, out_grad, expert_ids, combine, bucket_ids, w_gate, w_up, w_down):
     groups = lax.axis_size("blk")
     quads = lax.axis_size("quad")
@@ -312,8 +399,7 @@
     tokens, width = layer_input.shape
     capacity = 5 * tokens // (2 * experts)
     piece = width // groups
-    while groups * capacity % 16:
-        capacity += 1
+    capacity = -(-capacity // 8) * 8
     total = experts * capacity
 
     keys = jnp.concatenate([bucket_ids, expert_ids], axis=1)
@@ -337,11 +423,11 @@
     )
     send_x = dot(pick, layer_input, 1, 0).astype(BF16)
     send_w = (dot(pick, out_grad, 1, 0) * scale).astype(BF16)
-    both = ("quad", "blk")
-    rows_x = lax.all_to_all(send_x, both, split_axis=0, concat_axis=0, tiled=True)
-    rows_w = lax.all_to_all(send_w, both, split_axis=0, concat_axis=0, tiled=True)
-    rows_x = lax.all_gather(rows_x, SHARD, tiled=True)
-    rows_w = lax.all_gather(rows_w, SHARD, tiled=True)
+    chunk = (experts, capacity, width)
+    send = jnp.concatenate([send_x.reshape(chunk), send_w.reshape(chunk)], axis=1)
+    routed = dispatch(send, quads, groups)
+    rows_x = routed[:, :, :capacity].reshape(SHARDS * total, width)
+    rows_w = routed[:, :, capacity:].reshape(SHARDS * total, width)
 
     gate_w, up_w, down_w = w_gate[0, 0], w_up[0, 0], w_down[0, 0]
     gate = dot(rows_x, gate_w, 1, 0)

time: 265 us -> 258 us (0.974)
  Pallas kernels: 67.4 us -> 137 us
  blocking collectives: 139 us -> 70.7 us
  between operations: 14.4 us -> 0.97 us
  local copies, waits for them, and re-layouts: 0.12 us -> 10.9 us
  matrix products: 38.8 us -> 32.2 us
    all_to_all x2 -> x0, blocking collectives: 74.1 us -> none  [the longest x1 39.6 us: on_device(): lax.all_to_all(send_x, both, split_axis=0, concat_axis=0, tiled=True)]
    pallas_call x0 -> x1, Pallas kernels: none -> 68.5 us  [dispatch(): pl.pallas_call(functools.partial(dispatch_kernel, quads, groups), out_sha...]
    slice x0 -> x1, local copies, waits for them, and re-layouts: none -> 10.1 us  [on_device(): rows_w = routed[:, :, capacity:].reshape(SHARDS * total, width)]
    dot_general x12, matrix products: 37.8 us -> 31.2 us  [dot(): lax.dot_general(a, b, (((ca,), (cb,)), ((), ())), preferred_element_type=...]
    all_gather x1, blocking collectives: 65.1 us -> 70.7 us  [on_device(): all_keys = lax.all_gather(keys, ('quad', 'half', 'core', 'blk'), tiled=True)]
    pallas_call x1, Pallas kernels: 41.9 us -> 45.8 us  [return_rows(): pl.pallas_call(functools.partial(return_kernel, quads, groups), out_shape...]
  transfers between devices with their start and end apart: 2 -> 0, of which waited for: 0 -> 0; matrix products, arithmetic and copies ran while one was open for 5% -> 0% of each run, Pallas kernels for 0% -> 0%
where the time goes in v3:
time: 258 us
  Pallas kernels  137 us (53%)
  blocking collectives  70.7 us (27%)
  matrix products  32.2 us (12%)
  local copies, waits for them, and re-layouts  10.9 us (4%)
  other arithmetic  6 us (2%)
    all_gather x1, blocking collectives, on_device(): all_keys = lax.all_gather(keys, ('quad', 'half', 'core', 'blk'), tiled=True)  70.7 us
    pallas_call x1, Pallas kernels, dispatch(): pl.pallas_call(functools.partial(dispatch_kernel, quads, groups), out_sha...  68.5 us
    pallas_call x1, Pallas kernels, return_rows(): pl.pallas_call(functools.partial(return_kernel, quads, groups), out_shape...  45.8 us
    dot_general x12, matrix products, dot(): lax.dot_general(a, b, (((ca,), (cb,)), ((), ())), preferred_element_type=...  31.2 us
    pallas_call x1, Pallas kernels, gather_plane(): pl.pallas_call(functools.partial(gather_kernel, quads), out_shape=jax.Sha...  22.9 us
    slice x1, local copies, waits for them, and re-layouts, on_device(): rows_w = routed[:, :, capacity:].reshape(SHARDS * total, width)  10.1 us

profile of v3, /device:TPU:0, one launch (start us, length us, event | category | flops | bytes accessed | tf_op | source)
XLA Modules:
  0.0 258.0 jit_solution(5193725262877251442)
XLA Ops:
  0.7 0.8 fusion.59
  1.5 0.8 slice_bitcast_fusion.1
  2.5 0.7 convert_add_fusion
  3.4 0.7 pad_add_fusion
  4.1 70.7 %all_gather.3 = s32[4096,6]{0,1:T(8,128)S(1)} all-gather(s32[128,6]{0,1:T(8,128)S(1)} %pad_add_fusion), channel_id=1, replica_groups=mesh['quad'=2,'half'=2,'core'=2,'blk'=4] {'quad','half','core','blk'}, dimensions={0}, use_global_device_ids=true | all-gather | bytes 101376 | tf_op jit(solution)/shard_map/all_gather | solution.py:406
  75.1 0.2 fusion.29
  75.9 1.5 fusion
  77.5 0.5 convolution_convert_fusion.3
  78.0 1.8 pad_maximum_fusion.send
  79.8 1.5 bitcast_compare_fusion
  81.3 68.5 %dispatch.1 = bf16[4,8,80,2048]{3,2,1,0:T(8,128)(2,1)} custom-call(bf16[8,80,2048]{2,1,0:T(8,128)(2,1)} %pad_maximum_fusion.send), custom_call_target="tpu_custom_call" | custom-call | tf_op jit(solution)/shard_map/dispatch/pallas_call | solution.py:384
  149.8 10.1 %fusion.83 = (bf16[4,8,40,2048]{3,2,1,0:T(8,128)(2,1)}, bf16[4,8,40,2048]{3,2,1,0:T(8,128)(2,1)}) fusion(bf16[4,8,80,2048]{3,2,1,0:T(8,128)(2,1)} %dispatch.1), kind=kLoop, calls=%fused_computation.151 | loop fusion | bytes 20971520 | tf_op jit(solution)/shard_map/slice | solution.py:430
  160.0 4.7 %fusion.10 = f32[1280,352]{0,1:T(8,128)S(1)} fusion(bf16[1280,2048]{1,0:T(8,128)(2,1)} %bitcast.71, bf16[1,1,2048,352]{2,3,1,0:T(8,128)(2,1)S(1)} %copy-done), kind=kOutput, calls=%fused_computation.23 | convolution fusion | flops 1845493760 | bytes 8486912 | tf_op jit(solution)/shard_map/dot_general | solution.py:18
  164.7 2.1 fusion.13
  166.8 3.2 %fusion.4 = bf16[1,1,352,2048]{3,2,1,0:T(8,128)(2,1)} fusion(bf16[1280,2048]{1,0:T(8,128)(2,1)S(1)} %bitcast.77, f32[1280,352]{0,1:T(8,128)S(1)} %fusion.13, f32[1280,352]{0,1:T(8,128)S(1)} %fusion.10), kind=kOutput, calls=%fused_computation.13 | convolution fusion | flops 1848918016 | bytes 10289152 | tf_op jit(solution)/shard_map/dot_general | solution.py:18
  170.0 2.5 multiply_convert_fusion.1
  172.5 3.1 %fusion.6 = bf16[1,1,2048,352]{2,3,1,0:T(8,128)(2,1)} fusion(bf16[1280,352]{0,1:T(8,128)(2,1)S(1)} %get-tuple-element.10, bf16[1280,2048]{1,0:T(8,128)(2,1)S(1)} %bitcast.73), kind=kOutput, calls=%fused_computation.15 | convolution fusion | flops 1846214656 | bytes 7585792 | tf_op jit(solution)/shard_map/dot_general | solution.py:18
  175.7 3.1 %fusion.5 = bf16[1,1,2048,352]{2,3,1,0:T(8,128)(2,1)} fusion(bf16[1280,352]{0,1:T(8,128)(2,1)S(1)} %get-tuple-element.11, bf16[1280,2048]{1,0:T(8,128)(2,1)S(1)} %bitcast.74), kind=kOutput, calls=%fused_computation.14 | convolution fusion | flops 1846214656 | bytes 7585792 | tf_op jit(solution)/shard_map/dot_general | solution.py:18
  178.8 3.1 %fusion.8 = f32[1280,2048]{1,0:T(8,128)S(1)} fusion(bf16[1280,352]{0,1:T(8,128)(2,1)S(1)} %get-tuple-element.11, bf16[1,1,2048,352]{2,3,1,0:T(8,128)(2,1)S(1)} %copy-done), kind=kOutput, calls=%fused_computation.21 | convolution fusion | flops 1845493760 | bytes 12828672 | tf_op jit(solution)/shard_map/dot_general | solution.py:18
  181.9 3.1 %add_convert_fusion.part = bf16[1280,2048]{1,0:T(8,128)(2,1)S(1)} fusion(f32[1280,2048]{1,0:T(8,128)S(1)} %fusion.8, bf16[1280,352]{0,1:T(8,128)(2,1)S(1)} %get-tuple-element.10, bf16[1,1,2048,352]{2,3,1,0:T(8,128)(2,1)S(1)} %copy-done.3), kind=kOutput, calls=%fused_computation | convolution fusion | flops 1850736640 | bytes 18071552 | tf_op jit(solution)/shard_map/dot_general | solution.py:18
  185.1 45.8 %return_rows.1 = (bf16[8,160,512]{2,1,0:T(8,128)(2,1)S(1)}, bf16[4,128,512]{2,1,0:T(8,128)(2,1)S(1)}) custom-call(bf16[1280,2048]{1,0:T(8,128)(2,1)S(1)} %add_convert_fusion.part, bf16[128,2048]{1,0:T(8,128)(2,1)S(1)} %copy-done.1), custom_call_target="tpu_custom_call" | custom-call | tf_op jit(solution)/shard_map/return_rows/pallas_call | solution.py:182
  230.9 0.9 fusion.22.emb
  231.8 22.9 %gather_plane.1 = bf16[8,512,512]{2,1,0:T(8,128)(2,1)S(1)} custom-call(bf16[512,512]{1,0:T(8,128)(2,1)S(1)} %fusion.22.emb), custom_call_target="tpu_custom_call" | custom-call | tf_op jit(solution)/shard_map/gather_plane/pallas_call | solution.py:289
  254.7 3.3 %fusion.85 = f32[4,128,512]{2,1,0:T(8,128)} fusion(pred[4,128,4096]{2,1,0:T(32,128)(4,1)S(1)} %bitcast.81, bf16[4096,512,1]{1,0,2:T(8,128)(2,1)S(1)} %bitcast.68), kind=kOutput, calls=%fused_computation.153 | convolution fusion | flops 2147483648 | bytes 7340032 | tf_op jit(solution)/shard_map/dot_general | solution.py:18
  (42 shorter events, 1.3 us)
Async XLA Ops:
  0.6 159.3 %copy-start = (bf16[1,1,2048,352]{2,3,1,0:T(8,128)(2,1)S(1)}, bf16[1,1,2048,352]{2,3,1,0:T(8,128)(2,1)}, u32[]{:S(2)}) copy-start(bf16[1,1,2048,352]{2,3,1,0:T(8,128)(2,1)} %param.13) | copy-start | bytes 4325380
  0.6 76.8 %copy-start.4 = (bf16[128,2048]{1,0:T(8,128)(2,1)S(1)}, bf16[128,2048]{1,0:T(8,128)(2,1)}, u32[]{:S(2)}) copy-start(bf16[128,2048]{1,0:T(8,128)(2,1)} %param.8) | copy-start | bytes 1572868
  160.0 4.7 %copy-start.2 = (bf16[4,8,40,2048]{3,2,1,0:T(8,128)(2,1)S(1)}, bf16[4,8,40,2048]{3,2,1,0:T(8,128)(2,1)}, u32[]{:S(2)}) copy-start(bf16[4,8,40,2048]{3,2,1,0:T(8,128)(2,1)} %get-tuple-element.9) | copy-start | bytes 15728644
  160.0 4.7 %copy-start.3 = (bf16[1,1,2048,352]{2,3,1,0:T(8,128)(2,1)S(1)}, bf16[1,1,2048,352]{2,3,1,0:T(8,128)(2,1)}, u32[]{:S(2)}) copy-start(bf16[1,1,2048,352]{2,3,1,0:T(8,128)(2,1)} %param.14) | copy-start | bytes 4325380
  160.0 6.8 %slice-start = ((s8[5242880]{0:T(1024)(128)(4,1)}), s8[4194304]{0:T(1024)(128)(4,1)S(1)}, s32[]{:S(2)}) async-start(s8[5242880]{0:T(1024)(128)(4,1)} %bitcast.75), calls=%async_computation | async-start | bytes 8388608
  164.7 2.1 slice-start.1
  166.8 3.2 %copy-start.5 = (bf16[1,1,352,2048]{3,2,1,0:T(8,128)(2,1)S(1)}, bf16[1,1,352,2048]{3,2,1,0:T(8,128)(2,1)}, u32[]{:S(2)}) copy-start(bf16[1,1,352,2048]{3,2,1,0:T(8,128)(2,1)} %param.15) | copy-start | bytes 4325380
  181.9 3.2 %copy-start.1 = (bf16[128,2048]{1,0:T(8,128)(2,1)S(1)}, bf16[128,2048]{1,0:T(8,128)(2,1)}, u32[]{:S(2)}) copy-start(bf16[128,2048]{1,0:T(8,128)(2,1)} %grad.1) | copy-start | bytes 1572868
